TPU v7x, 32 devices: a whole 2x2x4 slice. The times are simulated.
32 devices in a mesh: replica: 8 (over y, x, core), shard: 4 (over z).
Axes of the slice: x: 2, y: 2, z: 4, core: 2. Of those that a mesh axis runs over, the one named last changes fastest.
Arguments:
- features: bfloat16 [8192, 8192], P(('replica', 'shard')), may hold values from -6 to 6
- key_grads: bfloat16 [8192, 1024], P(('replica', 'shard')), may hold values from -1.5 to 1.5
- key_weight: bfloat16 [8192, 1024], P('shard'), may hold values from -0.1875 to 0.1875
- momentum: float32 [8, 8192, 1024], P('replica', 'shard'), may hold values from -8 to 8
- worker_error: float32 [8, 8192, 1024], P('replica', 'shard'), may hold values from -2 to 2
- server_error: float32 [4, 2048, 1024], P('shard', 'replica'), may hold values from -2 to 2
Outputs:
- input_grads: bfloat16 [8192, 8192], P(('replica', 'shard'))
- synced_momentum: bfloat16 [8192, 1024], P('shard')
- new_worker_error: float32 [8, 8192, 1024], P('replica', 'shard')
- new_server_error: float32 [4, 2048, 1024], P('shard', 'replica')
All inputs are finite; a program needn't handle non-finite values. Where the computation divides by a largest or mean magnitude, that divisor is 1e-20 or more.
Results may differ from a plain program's by a relative error of at most 0.018.
Values may be sent and summed in bfloat16 or wider, within the bound.
A program may use at most 128 MiB of HBM per device.

v0:
```python
import jax
import jax.numpy as jnp
from jax import lax
from jax.sharding import PartitionSpec as P

decay_rate = 0.9


def compress(values):
    scale = jnp.mean(jnp.abs(values), axis=-1, keepdims=True) + 1e-06
    return (scale * jnp.tanh(values / scale)).astype(jnp.bfloat16)


def per_device(features, key_grads, key_weight, momentum, worker_error, server_error):
    shard_count = lax.axis_size("shard")
    replica_count = lax.axis_size("replica")
    local_rows = key_weight.shape[0]
    kv_width = key_weight.shape[1]
    all_grads = lax.all_gather(key_grads, "shard", axis=0, tiled=True)
    columns = lax.all_to_all(features, "shard", split_axis=1, concat_axis=0, tiled=True)
    tokens_dev = features.shape[0]
    col_blocks = columns.reshape(shard_count, tokens_dev, local_rows)
    grad_blocks = all_grads.reshape(shard_count, tokens_dev, kv_width)
    parts = jnp.einsum(
        "ntr,ntk->nrk", col_blocks, grad_blocks, preferred_element_type=jnp.float32
    ).astype(jnp.bfloat16)
    parts = lax.optimization_barrier(parts)
    weight_grad = jnp.sum(parts.astype(jnp.float32), axis=0)
    back_columns = lax.dot_general(
        all_grads, key_weight, (((1,), (1,)), ((), ())), preferred_element_type=jnp.float32
    ).astype(jnp.bfloat16)
    input_grads = lax.all_to_all(back_columns, "shard", split_axis=0, concat_axis=1, tiled=True)
    value = decay_rate * momentum[0] + (1.0 - decay_rate) * weight_grad + worker_error[0]
    packed = compress(value)
    new_worker = (value - packed.astype(jnp.float32))[None]
    received = lax.all_to_all(packed, "replica", split_axis=0, concat_axis=0, tiled=True)
    owned_rows = server_error.shape[1]
    stacked = received.reshape(replica_count, owned_rows, kv_width).astype(jnp.float32)
    held = jnp.sum(stacked, axis=0) / replica_count + server_error[0]
    synced_block = compress(held)
    new_server = (held - synced_block.astype(jnp.float32))[None]
    synced = lax.all_gather(synced_block, "replica", axis=0, tiled=True)
    return (input_grads, synced, new_worker, new_server)


def solution(mesh):
    in_specs = (
        P(("replica", "shard"), None),
        P(("replica", "shard"), None),
        P("shard", None),
        P("replica", "shard", None),
        P("replica", "shard", None),
        P("shard", "replica", None),
    )
    out_specs = (
        P(("replica", "shard"), None),
        P("shard", None),
        P("replica", "shard", None),
        P("shard", "replica", None),
    )
    return jax.shard_map(
        per_device, mesh=mesh, in_specs=in_specs, out_specs=out_specs, check_vma=False
    )
```

profile of v0, /device:TPU:27, one launch (start us, length us, event | category | flops | bytes accessed | tf_op | source)
XLA Modules:
  0.0 368.1 jit_solution(4118991228341156633)
XLA Ops:
  7.2 6.4 %copy.11 = bf16[256,8192]{0,1:T(8,128)(2,1)} copy(bf16[256,8192]{1,0:T(8,128)(2,1)} %param.6) | data formatting | bytes 8388608 | tf_op args[0]
  13.5 4.8 %all-to-all-start.1 = ((bf16[256,4,2048]{0,2,1:T(8,128)(2,1)}), bf16[256,4,2048]{0,2,1:T(8,128)(2,1)}, u32[]{:S(2)}, u32[]{:S(2)}) async-start(bf16[256,4,2048]{0,2,1:T(8,128)(2,1)} %bitcast.44), calls=%async_computation.1 | async-start | bytes 8388608 | tf_op jit(solution)/shard_map/all_to_all | solution.py:20
  18.4 0.0 all-gather.3.cloned.1.call-start
  18.4 0.7 all-gather.3.cloned.1.call-update
  19.1 0.0 all-gather.5.cloned.1.call-start
  19.2 108.7 %all-gather.3.cloned.1.call-done = bf16[1024,1024]{1,0:T(8,128)(2,1)} async-done(((bf16[256,1024]{1,0:T(8,128)(2,1)}), bf16[1024,1024]{1,0:T(8,128)(2,1)}) %all-gather.3.cloned.1.call-update) | async-done | bytes 2097168 | tf_op jit(solution)/shard_map/all_gather | solution.py:19
  127.9 14.6 %all-to-all-done.1 = bf16[256,4,2048]{0,2,1:T(8,128)(2,1)} async-done(((bf16[256,4,2048]{0,2,1:T(8,128)(2,1)}), bf16[256,4,2048]{0,2,1:T(8,128)(2,1)}, u32[]{:S(2)}, u32[]{:S(2)}) %all-to-all-start.1) | async-done | bytes 4194336 | tf_op jit(solution)/shard_map/all_to_all | solution.py:20
  142.5 13.1 %convolution_convert_fusion = bf16[4,2048,1024]{2,1,0:T(8,128)(2,1)} fusion(bf16[4,256,1024]{2,1,0:T(8,128)(2,1)} %bitcast.48, bf16[256,4,2048]{0,2,1:T(8,128)(2,1)} %all-to-all-done.1), kind=kOutput, calls=%fused_computation.1 | convolution fusion | flops 4303355904 | bytes 23068672 | tf_op jit(solution)/shard_map/ntr,ntk->nrk/dot_general | solution.py:24
  155.6 9.7 %convert_reduce_fusion = f32[2048,1024]{1,0:T(8,128)S(1)} fusion(bf16[4,2048,1024]{2,1,0:T(8,128)(2,1)} %convolution_convert_fusion), kind=kLoop, calls=%fused_computation | loop fusion | flops 14680064 | bytes 25165824 | tf_op jit(solution)/shard_map/reduce_sum | solution.py:28
  165.4 9.9 %fusion.2 = (f32[2048]{0:T(1024)S(1)}, f32[2048,1024]{1,0:T(8,128)}) fusion(f32[1,2048,1024]{2,1,0:T(8,128)} %param.10, f32[1,2048,1024]{2,1,0:T(8,128)} %param.9, f32[2048,1024]{1,0:T(8,128)S(1)} %convert_reduce_fusion), kind=kLoop, calls=%fused_computation.6 | loop fusion | flops 12580864 | bytes 33562624 | tf_op jit(solution)/shard_map/reduce_sum | solution.py:10
  175.2 10.8 %convert_subtract_fusion = (f32[1,2048,1024]{2,1,0:T(8,128)}, f32[1,2048,1024]{2,1,0:T(8,128)}) fusion(f32[1,2048,1024]{2,1,0:T(8,128)} %param.10, f32[2048]{0:T(1024)S(1)} %multiply_add_fusion, f32[1,2048,1024]{2,1,0:T(8,128)} %param.9, f32[2048,1024]{1,0:T(8,128)S(1)} %convert_reduce_fusion), kind=kLoop, calls=%fused_computation.8 | loop fusion | flops 18874368 | bytes 41951232 | tf_op jit(solution)/shard_map/sub | solution.py:35
  186.1 9.1 %multiply_convert_fusion.1 = bf16[8,256,1024]{2,1,0:T(8,128)(2,1)S(1)} fusion(f32[8,256,1024]{2,1,0:T(8,128)} %bitcast.41, f32[8,256,1024]{2,1,0:T(8,128)} %bitcast.43, f32[8,256,1024]{2,1,0:T(8,128)} %bitcast.42, f32[8,256]{1,0:T(8,128)S(1)} %add.54), kind=kLoop, calls=%fused_computation.11 | loop fusion | flops 10485760 | bytes 29368320 | tf_op jit(solution)/shard_map/convert_element_type | solution.py:11
  195.2 0.0 copy-start
  195.2 52.8 %all_to_all.41 = bf16[8,256,1024]{2,1,0:T(8,128)(2,1)S(1)} all-to-all(bf16[8,256,1024]{2,1,0:T(8,128)(2,1)S(1)} %multiply_convert_fusion.1), channel_id=1, replica_groups=mesh['replica'=8,'shard'=4] {'replica'}, dimensions={0} | all-to-all | bytes 8388608 | tf_op jit(solution)/shard_map/all_to_all | solution.py:36
  248.0 0.8 convert_reduce_fusion.1
  248.8 0.0 copy-done
  248.9 0.2 abs_reduce_fusion
  249.1 1.0 multiply_convert_fusion.3
  250.1 0.0 all-gather.5.cloned.1.call-update
  250.2 7.4 %convolution_convert_fusion.1 = bf16[1024,2048]{1,0:T(8,128)(2,1)S(1)} fusion(bf16[1024,1024]{1,0:T(8,128)(2,1)} %all-gather.3.cloned.1.call-done, bf16[2048,1024]{1,0:T(8,128)(2,1)} %param.8), kind=kOutput, calls=%fused_computation.15 | convolution fusion | flops 4297064448 | bytes 10485760 | tf_op jit(solution)/shard_map/dot_general | solution.py:29
  257.5 95.6 %all_to_all.42 = bf16[4,256,2048]{2,1,0:T(8,128)(2,1)S(1)} all-to-all(bf16[4,256,2048]{2,1,0:T(8,128)(2,1)S(1)} %bitcast.47), channel_id=1, replica_groups=mesh['replica'=8,'shard'=4] {'shard'}, dimensions={0} | all-to-all | bytes 8388608 | tf_op jit(solution)/shard_map/all_to_all | solution.py:32
  353.1 2.3 copy.12
  355.4 1.2 convert_subtract_fusion.1
  356.6 0.0 all-gather.5.cloned.1.call-done
  356.6 4.6 %copy.14 = bf16[2048,1024]{1,0:T(8,128)(2,1)} copy(bf16[2048,1024]{1,0:T(8,128)(2,1)} %all-gather.5.cloned.1.call-done) | data formatting | bytes 8388608
  (3 shorter events, 0.0 us)
Async XLA Ops:
  13.5 129.0 %all-to-all-start.1 = ((bf16[256,4,2048]{0,2,1:T(8,128)(2,1)}), bf16[256,4,2048]{0,2,1:T(8,128)(2,1)}, u32[]{:S(2)}, u32[]{:S(2)}) async-start(bf16[256,4,2048]{0,2,1:T(8,128)(2,1)} %bitcast.44), calls=%async_computation.1 | async-start | bytes 8388608 | tf_op jit(solution)/shard_map/all_to_all | solution.py:20
  18.4 109.5 %all-gather.3.cloned.1.call-start = ((), (), s32[]{:S(2)}) async-start(), calls=%async_computation.3 | async-start | bytes 2621440 | tf_op jit(solution)/shard_map/all_gather | solution.py:19
  19.1 337.5 %all-gather.5.cloned.1.call-start = ((), (), s32[]{:S(2)}) async-start(), calls=%async_computation.4 | async-start | bytes 4718592 | tf_op jit(solution)/shard_map/all_gather | solution.py:42
  195.2 53.7 %copy-start = (f32[1,256,1024]{2,1,0:T(8,128)S(1)}, f32[1,256,1024]{2,1,0:T(8,128)}, u32[]{:S(2)}) copy-start(f32[1,256,1024]{2,1,0:T(8,128)} %param.11) | copy-start | bytes 3145732
Sparse Core Ops, SparseCore 0:
  20.8 107.0 all-gather.2
  250.3 37.0 all-gather.4
where the time goes:
time: 373 us; the launch traced here: 368 us
  blocking collectives  148 us (40%)
  waiting for transfers between devices  124 us (33%)
  other arithmetic  42.9 us (12%)
  matrix products  20.5 us (5%)
  between operations  14.1 us (4%)
  local copies, waits for them, and re-layouts  13.3 us (4%)
  starting transfers between devices  4.92 us (1%)
    all_gather x1, waiting for transfers between devices, per_device(): all_grads = lax.all_gather(key_grads, 'shard', axis=0, tiled=True)  109 us
    all_to_all x1, blocking collectives, per_device(): lax.all_to_all(back_columns, 'shard', split_axis=0, concat_axis=1, tiled=...  95.6 us
    all_to_all x1, blocking collectives, per_device(): lax.all_to_all(packed, 'replica', split_axis=0, concat_axis=0, tiled=True)  52.8 us
    all_to_all x1, waiting for transfers between devices, per_device(): lax.all_to_all(features, 'shard', split_axis=1, concat_axis=0, tiled=True)  14.6 us
    dot_general x1, matrix products, per_device(): jnp.einsum('ntr,ntk->nrk', col_blocks, grad_blocks, preferred_element_typ...  13.1 us
    unnamed x4, local copies, waits for them, and re-layouts  11 us
    sub x1, other arithmetic, per_device(): new_worker = (value - packed.astype(jnp.float32))[None]  10.8 us
    convert_element_type x2, other arithmetic, compress(): return (scale * jnp.tanh(values / scale)).astype(jnp.bfloat16)  10.2 us
  transfers between devices with their start and end apart: 3, of which 2 were waited for; matrix products, arithmetic and copies ran while one was open for 3% of the time, Pallas kernels for 0%

commit v1 on v0

v1 whole, which is shorter than its diff:
```python
import functools

import jax
import jax.numpy as jnp
from jax import lax
from jax.experimental import pallas as pl
from jax.experimental.pallas import tpu as pltpu
from jax.sharding import PartitionSpec as P

decay_rate = 0.9


def compress(values):
    scale = jnp.mean(jnp.abs(values), axis=-1, keepdims=True) + 1e-06
    return (scale * jnp.tanh(values / scale)).astype(jnp.bfloat16)


def worker_kernel(cols_ref, grads_ref, moment_ref, error_ref, new_ref, packed_ref):
    grad = lax.dot_general(
        cols_ref[...], grads_ref[...], (((0,), (0,)), ((), ())), preferred_element_type=jnp.float32
    )
    value = decay_rate * moment_ref[0] + (1.0 - decay_rate) * grad + error_ref[0]
    packed = compress(value)
    new_ref[0] = value - packed.astype(jnp.float32)
    packed_ref[...] = packed


def worker_step(columns, all_grads, momentum, worker_error):
    tokens, rows = columns.shape
    width = all_grads.shape[1]
    chunk = min(256, rows)
    block = pl.BlockSpec((1, chunk, width), lambda i: (0, i, 0))
    return pl.pallas_call(
        worker_kernel,
        grid=(rows // chunk,),
        in_specs=[
            pl.BlockSpec((tokens, chunk), lambda i: (0, i)),
            pl.BlockSpec((tokens, width), lambda i: (0, 0)),
            block,
            block,
        ],
        out_specs=[block, pl.BlockSpec((chunk, width), lambda i: (i, 0))],
        out_shape=[
            jax.ShapeDtypeStruct(momentum.shape, jnp.float32),
            jax.ShapeDtypeStruct((rows, width), jnp.bfloat16),
        ],
        compiler_params=pltpu.CompilerParams(vmem_limit_bytes=40 * 2**20),
        cost_estimate=pl.CostEstimate(
            flops=2 * tokens * rows * width,
            bytes_accessed=14 * rows * width + 2 * tokens * (rows + width),
            transcendentals=rows * width,
        ),
    )(columns, all_grads, momentum, worker_error)


def per_device(features, key_grads, key_weight, momentum, worker_error, server_error):
    replica_count = lax.axis_size("replica")
    kv_width = key_weight.shape[1]
    share = key_weight.shape[0] // replica_count
    mine = lax.dynamic_slice_in_dim(key_weight, lax.axis_index("replica") * share, share, 0)
    all_grads = lax.all_gather(key_grads, "shard", axis=0, tiled=True)
    columns = lax.all_to_all(features, "shard", split_axis=1, concat_axis=0, tiled=True)
    all_weight = lax.all_gather(mine, ("shard", "replica"), axis=0, tiled=True)
    new_worker, packed = worker_step(columns, all_grads, momentum, worker_error)
    received = lax.all_to_all(packed, "replica", split_axis=0, concat_axis=0, tiled=True)
    owned_rows = server_error.shape[1]
    stacked = received.reshape(replica_count, owned_rows, kv_width).astype(jnp.float32)
    held = jnp.sum(stacked, axis=0) / replica_count + server_error[0]
    synced_block = compress(held)
    new_server = (held - synced_block.astype(jnp.float32))[None]
    synced = lax.all_gather(synced_block, "replica", axis=0, tiled=True)
    input_grads = lax.dot_general(
        key_grads, all_weight, (((1,), (1,)), ((), ())), preferred_element_type=jnp.float32
    ).astype(jnp.bfloat16)
    return (input_grads, synced, new_worker, new_server)


def solution(mesh):
    in_specs = (
        P(("replica", "shard"), None),
        P(("replica", "shard"), None),
        P("shard", None),
        P("replica", "shard", None),
        P("replica", "shard", None),
        P("shard", "replica", None),
    )
    out_specs = (
        P(("replica", "shard"), None),
        P("shard", None),
        P("replica", "shard", None),
        P("shard", "replica", None),
    )
    return jax.shard_map(
        per_device, mesh=mesh, in_specs=in_specs, out_specs=out_specs, check_vma=False
    )
```

time: 373 us -> 400 us (1.072)
  waiting for transfers between devices: 124 us -> 274 us
  blocking collectives: 148 us -> 52.7 us
  other arithmetic: 42.9 us -> 3.35 us
  Pallas kernels: 0 us -> 15 us
  matrix products: 20.5 us -> 12.4 us
  local copies, waits for them, and re-layouts: 13.3 us -> 19.6 us
    all_gather x0 -> x1, waiting for transfers between devices: none -> 116 us  [per_device(): all_weight = lax.all_gather(mine, ('shard', 'replica'), axis=0, tiled=True)]
    all_to_all x1 -> x0, blocking collectives: 95.6 us -> none  [per_device(): lax.all_to_all(back_columns, 'shard', split_axis=0, concat_axis=1, tiled=...]
    all_gather x1, waiting for transfers between devices: 0.01 us -> 34 us  [per_device(): synced = lax.all_gather(synced_block, 'replica', axis=0, tiled=True)]
    pallas_call x0 -> x1, Pallas kernels: none -> 15 us  [worker_step(): pl.pallas_call(worker_kernel, grid=(rows // chunk,), in_specs=[pl.BlockSp...]
    sub x1 -> x0, other arithmetic: 10.8 us -> none  [per_device(): new_worker = (value - packed.astype(jnp.float32))[None]]
    reduce_sum x2 -> x1, other arithmetic: 10.1 us -> 0.22 us  [compress(): scale = jnp.mean(jnp.abs(values), axis=-1, keepdims=True) + 1e-06]
    reduce_sum x1 -> x0, other arithmetic: 9.71 us -> none  [per_device(): weight_grad = jnp.sum(parts.astype(jnp.float32), axis=0)]
    convert_element_type x2 -> x1, other arithmetic: 10.2 us -> 1.04 us  [compress(): return (scale * jnp.tanh(values / scale)).astype(jnp.bfloat16)]
  transfers between devices with their start and end apart: 3 -> 4, of which waited for: 2 -> 4; matrix products, arithmetic and copies ran while one was open for 3% -> 1% of each run, Pallas kernels for 0% -> 0%
where the time goes in v1:
time: 400 us; the launch traced here: 396 us
  waiting for transfers between devices  274 us (68%)
  blocking collectives  52.7 us (13%)
  local copies, waits for them, and re-layouts  19.6 us (5%)
  Pallas kernels  15 us (4%)
  between operations  13.8 us (3%)
  matrix products  12.4 us (3%)
  starting transfers between devices  4.98 us (1%)
    all_gather x1, waiting for transfers between devices, per_device(): all_weight = lax.all_gather(mine, ('shard', 'replica'), axis=0, tiled=True)  116 us
    all_gather x1, waiting for transfers between devices, per_device(): all_grads = lax.all_gather(key_grads, 'shard', axis=0, tiled=True)  109 us
    all_to_all x1, blocking collectives, per_device(): lax.all_to_all(packed, 'replica', split_axis=0, concat_axis=0, tiled=True)  52.7 us
    all_gather x1, waiting for transfers between devices, per_device(): synced = lax.all_gather(synced_block, 'replica', axis=0, tiled=True)  34 us
    pallas_call x1, Pallas kernels, worker_step(): pl.pallas_call(worker_kernel, grid=(rows // chunk,), in_specs=[pl.BlockSp...  15 us
    all_to_all x1, waiting for transfers between devices, per_device(): lax.all_to_all(features, 'shard', split_axis=1, concat_axis=0, tiled=True)  14.5 us
    unnamed x8, local copies, waits for them, and re-layouts  12.9 us
    dot_general x1, matrix products, per_device(): lax.dot_general(key_grads, all_weight, (((1,), (1,)), ((), ())), preferre...  12.4 us
  transfers between devices with their start and end apart: 4, of which 4 were waited for; matrix products, arithmetic and copies ran while one was open for 1% of the time, Pallas kernels for 0%

profile of v1, /device:TPU:27, one launch (start us, length us, event | category | flops | bytes accessed | tf_op | source)
XLA Modules:
  0.0 396.0 jit_solution(953656037576949986)
XLA Ops:
  7.2 4.8 %copy.14 = bf16[32,4,8,2048]{3,2,0,1:T(8,128)(2,1)} copy(bf16[32,4,8,2048]{3,2,1,0:T(8,128)(2,1)} %bitcast.24) | data formatting | bytes 8388608 | tf_op jit(solution)/shard_map/all_to_all | solution.py:62
  12.0 4.9 %all-to-all-start = ((bf16[256,4,2048]{2,0,1:T(8,128)(2,1)}), bf16[256,4,2048]{2,0,1:T(8,128)(2,1)}, u32[]{:S(2)}, u32[]{:S(2)}) async-start(bf16[256,4,2048]{2,0,1:T(8,128)(2,1)} %bitcast.23), calls=%async_computation | async-start | bytes 8388608 | tf_op jit(solution)/shard_map/all_to_all | solution.py:62
  16.8 0.0 all-gather.6.cloned.1.call-start
  16.9 0.7 all-gather.6.cloned.1.call-update
  17.6 0.0 all-gather.8.cloned.1.call-start
  17.6 108.7 %all-gather.6.cloned.1.call-done.grads_ref = bf16[1024,1024]{1,0:T(8,128)(2,1)} async-done(((bf16[256,1024]{1,0:T(8,128)(2,1)}), bf16[1024,1024]{1,0:T(8,128)(2,1)}) %all-gather.6.cloned.1.call-update) | async-done | bytes 2097168 | tf_op jit(solution)/shard_map/all_gather | solution.py:61
  126.3 14.5 %all-to-all-done = bf16[256,4,2048]{2,0,1:T(8,128)(2,1)} async-done(((bf16[256,4,2048]{2,0,1:T(8,128)(2,1)}), bf16[256,4,2048]{2,0,1:T(8,128)(2,1)}, u32[]{:S(2)}, u32[]{:S(2)}) %all-to-all-start) | async-done | bytes 4194336 | tf_op jit(solution)/shard_map/all_to_all | solution.py:62
  140.9 0.0 copy-start
  140.9 1.6 copy-done
  142.5 15.0 %shard_map.93 = (f32[1,2048,1024]{2,1,0:T(8,128)}, bf16[2048,1024]{1,0:T(8,128)(2,1)S(1)}) custom-call(bf16[1024,2048]{1,0:T(8,128)(2,1)} %bitcast.2.cols_ref, bf16[1024,1024]{1,0:T(8,128)(2,1)S(1)} %copy-done, f32[1,2048,1024]{2,1,0:T(8,128)} %moment_ref.1, f32[1,2048,1024]{2,1,0:T(8,128)} %error_ref.1), custom_call_target="tpu_custom_call" | custom-call | flops 4294967296 | bytes 35651584 | tf_op jit(solution)/shard_map/pallas_call | solution.py:33
  157.5 52.7 %all_to_all.28 = bf16[8,256,1024]{2,1,0:T(8,128)(2,1)S(1)} all-to-all(bf16[8,256,1024]{2,1,0:T(8,128)(2,1)S(1)} %bitcast.22), channel_id=1, replica_groups=mesh['replica'=8,'shard'=4] {'replica'}, dimensions={0} | all-to-all | bytes 8388608 | tf_op jit(solution)/shard_map/all_to_all | solution.py:65
  210.2 0.0 copy-start.1
  210.2 0.9 convert_reduce_fusion
  211.1 0.4 copy-done.1
  211.4 0.2 abs_reduce_fusion
  211.6 0.0 copy-start.2
  211.7 1.0 multiply_convert_fusion.1
  212.7 0.0 all-gather.8.cloned.1.call-update
  212.7 0.0 all-gather.4.cloned.1.call-start
  212.8 1.9 constant_dynamic-slice_fusion
  214.7 0.0 all-gather.4.cloned.1.call-update
  214.7 1.2 convert_subtract_fusion
  215.9 34.0 %all-gather.8.cloned.1.call-done = bf16[2048,1024]{1,0:T(8,128)(2,1)} async-done(((bf16[256,1024]{1,0:T(8,128)(2,1)}), bf16[2048,1024]{1,0:T(8,128)(2,1)}) %all-gather.8.cloned.1.call-update) | async-done | bytes 4194320 | tf_op jit(solution)/shard_map/all_gather | solution.py:71
  249.9 116.2 %all-gather.4.cloned.1.call-done = bf16[8192,1024]{1,0:T(8,128)(2,1)} async-done(((bf16[256,1024]{1,0:T(8,128)(2,1)}), bf16[8192,1024]{1,0:T(8,128)(2,1)}) %all-gather.4.cloned.1.call-update) | async-done | bytes 16777232 | tf_op jit(solution)/shard_map/all_gather | solution.py:63
  366.2 0.0 copy-done.2
  366.2 12.4 %fusion = bf16[256,8192]{0,1:T(8,128)(2,1)} fusion(bf16[8192,1024]{1,0:T(8,128)(2,1)} %all-gather.4.cloned.1.call-done, bf16[256,1024]{1,0:T(8,128)(2,1)S(1)} %copy-done.2), kind=kOutput, calls=%fused_computation.1 | convolution fusion | flops 4297064448 | bytes 21495808 | tf_op jit(solution)/shard_map/dot_general | solution.py:72
  378.5 6.3 %copy.11 = bf16[256,8192]{1,0:T(8,128)(2,1)} copy(bf16[256,8192]{0,1:T(8,128)(2,1)} %fusion) | data formatting | bytes 8388608
  384.8 4.6 %copy.16 = bf16[2048,1024]{1,0:T(8,128)(2,1)} copy(bf16[2048,1024]{1,0:T(8,128)(2,1)} %all-gather.8.cloned.1.call-done) | data formatting | bytes 8388608
  (1 shorter events, 0.0 us)
Async XLA Ops:
  12.0 128.9 %all-to-all-start = ((bf16[256,4,2048]{2,0,1:T(8,128)(2,1)}), bf16[256,4,2048]{2,0,1:T(8,128)(2,1)}, u32[]{:S(2)}, u32[]{:S(2)}) async-start(bf16[256,4,2048]{2,0,1:T(8,128)(2,1)} %bitcast.23), calls=%async_computation | async-start | bytes 8388608 | tf_op jit(solution)/shard_map/all_to_all | solution.py:62
  16.8 109.5 %all-gather.6.cloned.1.call-start = ((), (), s32[]{:S(2)}) async-start(), calls=%async_computation.3 | async-start | bytes 2621440 | tf_op jit(solution)/shard_map/all_gather | solution.py:61
  17.6 232.4 %all-gather.8.cloned.1.call-start = ((), (), s32[]{:S(2)}) async-start(), calls=%async_computation.4 | async-start | bytes 4718592 | tf_op jit(solution)/shard_map/all_gather | solution.py:71
  140.9 1.6 copy-start
  210.2 1.2 copy-start.1
  211.6 154.5 %copy-start.2 = (bf16[256,1024]{1,0:T(8,128)(2,1)S(1)}, bf16[256,1024]{1,0:T(8,128)(2,1)}, u32[]{:S(2)}) copy-start(bf16[256,1024]{1,0:T(8,128)(2,1)} %param.7) | copy-start | bytes 1572868
  212.7 153.4 %all-gather.4.cloned.1.call-start = ((), (), s32[]{:S(2)}) async-start(), calls=%async_computation.2 | async-start | bytes 17301504 | tf_op jit(solution)/shard_map/all_gather | solution.py:63
Sparse Core Ops, SparseCore 0:
  19.2 107.0 all-gather.5
  212.8 37.0 all-gather.7
  253.4 112.7 all-gather.3

commit v2 on v0

v2 whole, which is shorter than its diff:
```python
import functools

import jax
import jax.numpy as jnp
from jax import lax
from jax.experimental import pallas as pl
from jax.experimental.pallas import tpu as pltpu
from jax.sharding import PartitionSpec as P

MESH = pl.DeviceIdType.MESH

decay_rate = 0.9


def compress(values):
    scale = jnp.mean(jnp.abs(values), axis=-1, keepdims=True) + 1e-06
    return (scale * jnp.tanh(values / scale)).astype(jnp.bfloat16)


def exchange_kernel(
    shards, replicas, features, grads, weight, moment, error, server,
    input_grads, synced, new_worker, new_server,
    block, held_weight, back, cols, all_grads, mom, err, packed, got, total,
    grad_local, grad_send, grad_recv, load, col_send, col_recv, store, pack_send, pack_recv,
    weight_load, back_local, back_send, back_recv, sync_local, sync_send, sync_recv,
):
    r, s = lax.axis_index("replica"), lax.axis_index("shard")
    tokens = grads.shape[0]
    chunks, rows = mom.shape[0], mom.shape[1]
    owned = got.shape[1]
    per = rows // owned
    shard_rows = chunks * rows
    first = r // per + 1

    barrier = pltpu.get_barrier_semaphore()
    for d in range(1, shards):
        pl.semaphore_signal(barrier, inc=1, device_id=(r, lax.rem(s + d, shards)), device_id_type=MESH)
    for d in range(1, replicas):
        pl.semaphore_signal(barrier, inc=1, device_id=(lax.rem(r + d, replicas), s), device_id_type=MESH)
    pl.semaphore_wait(barrier, shards + replicas - 2)

    def grad_copy(d):
        return pltpu.make_async_remote_copy(
            src_ref=grads,
            dst_ref=all_grads.at[pl.ds(d * tokens, tokens)],
            send_sem=grad_send.at[d],
            recv_sem=grad_recv.at[d],
            device_id=(r, lax.rem(s + d, shards)),
            device_id_type=MESH,
        )

    def columns_of(owner, c):
        return features.at[:, pl.ds(pl.multiple_of((owner * chunks + c) * rows, 128), rows)]

    def col_copy(d, c):
        dest = lax.rem(s + d, shards)
        return pltpu.make_async_remote_copy(
            src_ref=columns_of(dest, c),
            dst_ref=cols.at[c, pl.ds(d * tokens, tokens)],
            send_sem=col_send.at[d, c],
            recv_sem=col_recv.at[d, c],
            device_id=(r, dest),
            device_id_type=MESH,
        )

    def loads(c):
        here = pl.ds(pl.multiple_of(c * rows, 16), rows)
        return (
            pltpu.make_async_copy(columns_of(s, c), cols.at[c, pl.ds(0, tokens)], load.at[0, c]),
            pltpu.make_async_copy(moment.at[0, here], mom.at[c], load.at[1, c]),
            pltpu.make_async_copy(error.at[0, here], err.at[c], load.at[2, c]),
        )

    def store_copy(c):
        here = pl.ds(pl.multiple_of(c * rows, 16), rows)
        return pltpu.make_async_copy(mom.at[c], new_worker.at[0, here], store.at[c])

    def pack_copy(c, q):
        owner = c * per + q
        return pltpu.make_async_remote_copy(
            src_ref=packed.at[c, pl.ds(q * owned, owned)],
            dst_ref=got.at[r],
            send_sem=pack_send.at[owner],
            recv_sem=pack_recv.at[r],
            device_id=(owner, s),
            device_id_type=MESH,
        )

    def back_copy(d):
        return pltpu.make_async_remote_copy(
            src_ref=back.at[d],
            dst_ref=input_grads.at[:, pl.ds(pl.multiple_of(s * shard_rows, 128), shard_rows)],
            send_sem=back_send.at[d],
            recv_sem=back_recv.at[d],
            device_id=(r, lax.rem(s + shards - d, shards)),
            device_id_type=MESH,
        )

    def back_arrival(d):
        source = lax.rem(s + d, shards)
        return pltpu.make_async_remote_copy(
            src_ref=back.at[d],
            dst_ref=input_grads.at[:, pl.ds(pl.multiple_of(source * shard_rows, 128), shard_rows)],
            send_sem=back_send.at[d],
            recv_sem=back_recv.at[d],
            device_id=(r, source),
            device_id_type=MESH,
        )

    own_back = pltpu.make_async_copy(
        back.at[0],
        input_grads.at[:, pl.ds(pl.multiple_of(s * shard_rows, 128), shard_rows)],
        back_local,
    )

    def sync_copy(j, place):
        return pltpu.make_async_remote_copy(
            src_ref=block,
            dst_ref=synced.at[pl.ds(pl.multiple_of(place * owned, 16), owned)],
            send_sem=sync_send.at[j],
            recv_sem=sync_recv.at[j],
            device_id=(lax.rem(r + j, replicas), s),
            device_id_type=MESH,
        )

    own_block = pltpu.make_async_copy(
        block, synced.at[pl.ds(pl.multiple_of(r * owned, 16), owned)], sync_local
    )
    load_weight = pltpu.make_async_copy(weight, held_weight, weight_load)
    load_weight.start()
    own_grads = pltpu.make_async_copy(grads, all_grads.at[pl.ds(0, tokens)], grad_local)
    own_grads.start()
    for d in range(1, shards):
        grad_copy(d).start()

    @pl.loop(0, chunks)
    def _(k):
        c = lax.rem(first + k, chunks)
        for d in range(1, shards):
            col_copy(d, c).start()
        for copy in loads(c):
            copy.start()

    own_grads.wait()
    for d in range(1, shards):
        grad_copy(d).wait_recv()
    load_weight.wait()

    @pl.loop(0, chunks)
    def _(c):
        here = pl.ds(pl.multiple_of(c * rows, 128), rows)
        product = lax.dot_general(
            all_grads[...], held_weight[here, :], (((1,), (1,)), ((), ())),
            preferred_element_type=jnp.float32,
        ).astype(jnp.bfloat16)
        for d in range(shards):
            back[d, :, here] = product[d * tokens:(d + 1) * tokens]

    own_back.start()
    for d in range(1, shards):
        back_copy(d).start()

    @pl.loop(0, chunks)
    def _(k):
        c = lax.rem(first + k, chunks)
        for copy in loads(c):
            copy.wait()
        for d in range(1, shards):
            col_copy(d, c).wait_recv()
        grad = lax.dot_general(
            cols[c], all_grads[...], (((0,), (0,)), ((), ())), preferred_element_type=jnp.float32
        )
        value = decay_rate * mom[c] + (1.0 - decay_rate) * grad + err[c]
        small = compress(value)
        mom[c] = value - small.astype(jnp.float32)
        packed[c] = small
        for q in range(per):
            @pl.when(c * per + q != r)
            def _():
                pack_copy(c, q).start()
        store_copy(c).start()

    mine = packed[r // per, pl.ds(pl.multiple_of(lax.rem(r, per) * owned, 16), owned)]
    total[...] = mine.astype(jnp.float32)

    @pl.loop(1, replicas)
    def _(j):
        source = lax.rem(r + j, replicas)
        pltpu.make_async_remote_copy(
            src_ref=packed.at[0, pl.ds(0, owned)],
            dst_ref=got.at[source],
            send_sem=pack_send.at[source],
            recv_sem=pack_recv.at[source],
            device_id=(source, s),
            device_id_type=MESH,
        ).wait_recv()
        total[...] += got[source].astype(jnp.float32)

    held = total[...] / replicas + server[0]
    average = compress(held)
    new_server[0] = held - average.astype(jnp.float32)
    block[...] = average
    own_block.start()

    @pl.loop(1, replicas)
    def _(j):
        sync_copy(j, r).start()

    for d in range(1, shards):
        grad_copy(d).wait_send()

    @pl.loop(0, chunks)
    def _(c):
        for d in range(1, shards):
            col_copy(d, c).wait_send()
        for q in range(per):
            @pl.when(c * per + q != r)
            def _():
                pack_copy(c, q).wait_send()
        store_copy(c).wait()

    own_back.wait()
    own_block.wait()
    for d in range(1, shards):
        back_copy(d).wait_send()
        back_arrival(d).wait_recv()

    @pl.loop(1, replicas)
    def _(j):
        sync_copy(j, r).wait_send()
        sync_copy(j, lax.rem(r + replicas - j, replicas)).wait_recv()


def exchange(features, key_grads, key_weight, momentum, worker_error, server_error):
    shards, replicas = lax.axis_size("shard"), lax.axis_size("replica")
    tokens, width = key_grads.shape
    shard_rows = momentum.shape[1]
    owned = server_error.shape[1]
    rows = owned * max(1, 256 // owned)
    chunks = shard_rows // rows
    any_space = pl.BlockSpec(memory_space=pl.ANY)
    vmem = pl.BlockSpec(memory_space=pltpu.VMEM)
    dma = pltpu.SemaphoreType.DMA
    bf16, f32 = jnp.bfloat16, jnp.float32
    return pl.pallas_call(
        functools.partial(exchange_kernel, shards, replicas),
        in_specs=[any_space] * 5 + [vmem],
        out_specs=[any_space] * 3 + [vmem],
        out_shape=[
            jax.ShapeDtypeStruct(features.shape, bf16),
            jax.ShapeDtypeStruct(key_weight.shape, bf16),
            jax.ShapeDtypeStruct(momentum.shape, f32),
            jax.ShapeDtypeStruct(server_error.shape, f32),
        ],
        scratch_shapes=[
            pltpu.VMEM((owned, width), bf16),
            pltpu.VMEM((shard_rows, width), bf16),
            pltpu.VMEM((shards, tokens, shard_rows), bf16),
            pltpu.VMEM((chunks, shards * tokens, rows), bf16),
            pltpu.VMEM((shards * tokens, width), bf16),
            pltpu.VMEM((chunks, rows, width), f32),
            pltpu.VMEM((chunks, rows, width), f32),
            pltpu.VMEM((chunks, rows, width), bf16),
            pltpu.VMEM((replicas, owned, width), bf16),
            pltpu.VMEM((owned, width), f32),
            dma(()),
            dma((shards,)),
            dma((shards,)),
            dma((3, chunks)),
            dma((shards, chunks)),
            dma((shards, chunks)),
            dma((chunks,)),
            dma((replicas,)),
            dma((replicas,)),
            dma(()),
            dma(()),
            dma((shards,)),
            dma((shards,)),
            dma(()),
            dma((replicas,)),
            dma((replicas,)),
        ],
        compiler_params=pltpu.CompilerParams(
            collective_id=0, has_side_effects=True, vmem_limit_bytes=58 * 2**20
        ),
        cost_estimate=pl.CostEstimate(
            flops=2 * tokens * shards * shard_rows * width,
            bytes_accessed=40 * 2 * tokens * shards * (shard_rows + width),
            transcendentals=shard_rows * width,
        ),
    )(features, key_grads, key_weight, momentum, worker_error, server_error)


def per_device(features, key_grads, key_weight, momentum, worker_error, server_error):
    return tuple(
        exchange(features, key_grads, key_weight, momentum, worker_error, server_error)
    )


def solution(mesh):
    in_specs = (
        P(("replica", "shard"), None),
        P(("replica", "shard"), None),
        P("shard", None),
        P("replica", "shard", None),
        P("replica", "shard", None),
        P("shard", "replica", None),
    )
    out_specs = (
        P(("replica", "shard"), None),
        P("shard", None),
        P("replica", "shard", None),
        P("shard", "replica", None),
    )
    return jax.shard_map(
        per_device, mesh=mesh, in_specs=in_specs, out_specs=out_specs, check_vma=False
    )
```

time: 373 us -> 266 us (0.71); the launches traced: 368 us -> 266 us
  Pallas kernels: 0 us -> 251 us
  blocking collectives: 148 us -> 0 us
  waiting for transfers between devices: 124 us -> 0 us
  other arithmetic: 42.9 us -> 0.01 us
  matrix products: 20.5 us -> 0 us
  between operations: 14.1 us -> 0.66 us
  starting transfers between devices: 4.92 us -> 0 us
    pallas_call x0 -> x1, Pallas kernels: none -> 251 us  [exchange(): pl.pallas_call(functools.partial(exchange_kernel, shards, replicas), in_s...]
    all_to_all x2 -> x0, blocking collectives: 148 us -> none  [the longest x1 95.6 us: per_device(): lax.all_to_all(back_columns, 'shard', split_axis=0, concat_axis=1, tiled=...]
    all_gather x2 -> x0, waiting for transfers between devices: 109 us -> none  [the longest x1 109 us: per_device(): all_grads = lax.all_gather(key_grads, 'shard', axis=0, tiled=True)]
    reduce_sum x4 -> x0, other arithmetic: 20.6 us -> none  [the longest x2 10.1 us: compress(): scale = jnp.mean(jnp.abs(values), axis=-1, keepdims=True) + 1e-06]
    dot_general x2 -> x0, matrix products: 20.5 us -> none  [the longest x1 13.1 us: per_device(): jnp.einsum('ntr,ntk->nrk', col_blocks, grad_blocks, preferred_element_typ...]
    all_to_all x1 -> x0, waiting for transfers between devices: 14.6 us -> none  [per_device(): lax.all_to_all(features, 'shard', split_axis=1, concat_axis=0, tiled=True)]
    sub x2 -> x0, other arithmetic: 12.1 us -> none  [the longest x1 10.8 us: per_device(): new_worker = (value - packed.astype(jnp.float32))[None]]
    convert_element_type x2 -> x0, other arithmetic: 10.2 us -> none  [compress(): return (scale * jnp.tanh(values / scale)).astype(jnp.bfloat16)]
  transfers between devices with their start and end apart: 3 -> 0, of which waited for: 2 -> 0; matrix products, arithmetic and copies ran while one was open for 3% -> 0% of each run, Pallas kernels for 0% -> 0%
where the time goes in v2:
time: 266 us
  Pallas kernels  251 us (94%)
  local copies, waits for them, and re-layouts  13.5 us (5%)
    pallas_call x1, Pallas kernels, exchange(): pl.pallas_call(functools.partial(exchange_kernel, shards, replicas), in_s...  251 us
    unnamed x12, local copies, waits for them, and re-layouts  13.5 us

profile of v2, /device:TPU:27, one launch (start us, length us, event | category | flops | bytes accessed | tf_op | source)
XLA Modules:
  0.0 265.6 jit_solution(11450543150251724975)
XLA Ops:
  0.6 251.4 %shard_map.93 = (bf16[256,8192]{1,0:T(8,128)(2,1)}, bf16[2048,1024]{1,0:T(8,128)(2,1)}, f32[1,2048,1024]{2,1,0:T(8,128)}, f32[1,256,1024]{2,1,0:T(8,128)}) custom-call(bf16[256,8192]{1,0:T(8,128)(2,1)} %features.1, bf16[256,1024]{1,0:T(8,128)(2,1)} %grads.1, bf16[2048,1024]{1,0:T(8,128)(2,1)} %weight.1, f32[1,2048,1024]{2,1,0:T(8,128)} %moment.1, ...), custom_call_target="tpu_custom_call" | custom-call | flops 4294967296 | bytes 251658240 | tf_op jit(solution)/shard_map/pallas_call | solution.py:245
  252.1 0.0 copy-start
  252.1 0.0 slice-start
  252.1 4.9 %copy.14 = bf16[256,8192]{1,0:T(8,128)(2,1)} copy(bf16[256,8192]{1,0:T(8,128)(2,1)} %get-tuple-element.8) | data formatting | bytes 8388608
  257.0 0.0 copy-done
  257.0 0.0 slice-start.1
  257.0 2.1 copy.15
  259.1 0.0 slice-done
  259.1 2.1 slice-done.1
  261.2 0.0 copy-start.1
  261.2 3.4 %copy.16 = f32[1,2048,1024]{2,1,0:T(8,128)} copy(f32[1,2048,1024]{2,1,0:T(8,128)S(1)} %bitcast.1) | data formatting | bytes 16777216
  264.6 0.0 copy-done.1
  264.6 1.0 copy.17
  (1 shorter events, 0.0 us)
Async XLA Ops:
  252.1 4.9 %copy-start = (bf16[2048,1024]{1,0:T(8,128)(2,1)S(1)}, bf16[2048,1024]{1,0:T(8,128)(2,1)}, u32[]{:S(2)}) copy-start(bf16[2048,1024]{1,0:T(8,128)(2,1)} %get-tuple-element.9) | copy-start | bytes 12582916
  252.1 7.1 %slice-start = ((s8[8388608]{0:T(1024)(128)(4,1)}), s8[4194304]{0:T(1024)(128)(4,1)S(1)}, s32[]{:S(2)}) async-start(s8[8388608]{0:T(1024)(128)(4,1)} %bitcast), calls=%async_computation | async-start | bytes 8388608
  257.0 4.2 %slice-start.1 = ((s8[8388608]{0:T(1024)(128)(4,1)}), s8[4194304]{0:T(1024)(128)(4,1)S(1)}, s32[]{:S(2)}) async-start(s8[8388608]{0:T(1024)(128)(4,1)} %bitcast), calls=%async_computation.1 | async-start | bytes 8388608
  261.2 3.4 %copy-start.1 = (f32[1,256,1024]{2,1,0:T(8,128)S(1)}, f32[1,256,1024]{2,1,0:T(8,128)}, u32[]{:S(2)}) copy-start(f32[1,256,1024]{2,1,0:T(8,128)} %get-tuple-element.11) | copy-start | bytes 3145732

commit v3 on v2

--- a/solution.py
+++ b/solution.py
@@ -22,7 +22,7 @@
     input_grads, synced, new_worker, new_server,
     block, held_weight, back, cols, all_grads, mom, err, packed, got, total,
     grad_local, grad_send, grad_recv, load, col_send, col_recv, store, pack_send, pack_recv,
-    weight_load, back_local, back_send, back_recv, sync_local, sync_send, sync_recv,
+    weight_load, back_local, far_send, far_recv, plane_send, plane_recv, pair_send, pair_recv, sync_local, sync_send, sync_recv,
 ):
     r, s = lax.axis_index("replica"), lax.axis_index("shard")
     tokens = grads.shape[0]
@@ -86,32 +86,46 @@
             device_id_type=MESH,
         )
 
-    def back_copy(d):
-        return pltpu.make_async_remote_copy(
-            src_ref=back.at[d],
-            dst_ref=input_grads.at[:, pl.ds(pl.multiple_of(s * shard_rows, 128), shard_rows)],
-            send_sem=back_send.at[d],
-            recv_sem=back_recv.at[d],
-            device_id=(r, lax.rem(s + shards - d, shards)),
-            device_id_type=MESH,
-        )
-
-    def back_arrival(d):
-        source = lax.rem(s + d, shards)
-        return pltpu.make_async_remote_copy(
-            src_ref=back.at[d],
-            dst_ref=input_grads.at[:, pl.ds(pl.multiple_of(source * shard_rows, 128), shard_rows)],
-            send_sem=back_send.at[d],
-            recv_sem=back_recv.at[d],
-            device_id=(r, source),
-            device_id_type=MESH,
-        )
-
-    own_back = pltpu.make_async_copy(
-        back.at[0],
-        input_grads.at[:, pl.ds(pl.multiple_of(s * shard_rows, 128), shard_rows)],
-        back_local,
-    )
+    half = replicas // 2
+    partner = r + 1 - 2 * lax.rem(r, 2)
+
+    def piece(shard, replica):
+        start = shard * shard_rows + replica * owned
+        return held_weight.at[pl.ds(pl.multiple_of(start, 16), owned)]
+
+    def far_copy(d):
+        return pltpu.make_async_remote_copy(
+            src_ref=weight.at[pl.ds(pl.multiple_of(r * owned, 16), owned)],
+            dst_ref=piece(s, r),
+            send_sem=far_send.at[d],
+            recv_sem=far_recv.at[d],
+            device_id=(r, lax.rem(s + d, shards)),
+            device_id_type=MESH,
+        )
+
+    def plane_copy(d, j):
+        mine = piece(lax.rem(s + shards - d, shards), r)
+        return pltpu.make_async_remote_copy(
+            src_ref=mine,
+            dst_ref=mine,
+            send_sem=plane_send.at[d, j],
+            recv_sem=plane_recv.at[d, j],
+            device_id=(lax.rem(r + 2 * j, replicas), s),
+            device_id_type=MESH,
+        )
+
+    def pair_copy(d, j):
+        here = piece(lax.rem(s + shards - d, shards), lax.rem(r + replicas - 2 * j, replicas))
+        return pltpu.make_async_remote_copy(
+            src_ref=here,
+            dst_ref=here,
+            send_sem=pair_send.at[d, j],
+            recv_sem=pair_recv.at[d, j],
+            device_id=(partner, s),
+            device_id_type=MESH,
+        )
+
+    own_back = pltpu.make_async_copy(back, input_grads, back_local)
 
     def sync_copy(j, place):
         return pltpu.make_async_remote_copy(
@@ -126,12 +140,16 @@
     own_block = pltpu.make_async_copy(
         block, synced.at[pl.ds(pl.multiple_of(r * owned, 16), owned)], sync_local
     )
-    load_weight = pltpu.make_async_copy(weight, held_weight, weight_load)
+    load_weight = pltpu.make_async_copy(
+        weight, held_weight.at[pl.ds(pl.multiple_of(s * shard_rows, 16), shard_rows)], weight_load
+    )
     load_weight.start()
     own_grads = pltpu.make_async_copy(grads, all_grads.at[pl.ds(0, tokens)], grad_local)
     own_grads.start()
     for d in range(1, shards):
         grad_copy(d).start()
+    for d in range(1, shards):
+        far_copy(d).start()
 
     @pl.loop(0, chunks)
     def _(k):
@@ -144,21 +162,12 @@
     own_grads.wait()
     for d in range(1, shards):
         grad_copy(d).wait_recv()
-    load_weight.wait()
-
-    @pl.loop(0, chunks)
-    def _(c):
-        here = pl.ds(pl.multiple_of(c * rows, 128), rows)
-        product = lax.dot_general(
-            all_grads[...], held_weight[here, :], (((1,), (1,)), ((), ())),
-            preferred_element_type=jnp.float32,
-        ).astype(jnp.bfloat16)
-        for d in range(shards):
-            back[d, :, here] = product[d * tokens:(d + 1) * tokens]
-
-    own_back.start()
-    for d in range(1, shards):
-        back_copy(d).start()
+    for d in range(1, shards):
+        far_copy(d).wait_recv()
+
+        @pl.loop(1, half)
+        def _(j):
+            plane_copy(d, j).start()
 
     @pl.loop(0, chunks)
     def _(k):
@@ -180,6 +189,14 @@
                 pack_copy(c, q).start()
         store_copy(c).start()
 
+    for d in range(1, shards):
+        pair_copy(d, 0).start()
+
+        @pl.loop(1, half)
+        def _(j):
+            plane_copy(d, j).wait_recv()
+            pair_copy(d, j).start()
+
     mine = packed[r // per, pl.ds(pl.multiple_of(lax.rem(r, per) * owned, 16), owned)]
     total[...] = mine.astype(jnp.float32)
 
@@ -206,6 +223,22 @@
     def _(j):
         sync_copy(j, r).start()
 
+    load_weight.wait()
+    for d in range(1, shards):
+        @pl.loop(0, half)
+        def _(j):
+            pair_copy(d, j).wait_recv()
+
+    @pl.loop(0, shards * chunks)
+    def _(i):
+        here = pl.ds(pl.multiple_of(i * rows, 128), rows)
+        back[:, here] = lax.dot_general(
+            all_grads[0:tokens], held_weight[here, :], (((1,), (1,)), ((), ())),
+            preferred_element_type=jnp.float32,
+        ).astype(jnp.bfloat16)
+
+    own_back.start()
+
     for d in range(1, shards):
         grad_copy(d).wait_send()
 
@@ -222,8 +255,15 @@
     own_back.wait()
     own_block.wait()
     for d in range(1, shards):
-        back_copy(d).wait_send()
-        back_arrival(d).wait_recv()
+        far_copy(d).wait_send()
+
+        @pl.loop(1, half)
+        def _(j):
+            plane_copy(d, j).wait_send()
+
+        @pl.loop(0, half)
+        def _(j):
+            pair_copy(d, j).wait_send()
 
     @pl.loop(1, replicas)
     def _(j):
@@ -254,8 +294,8 @@
         ],
         scratch_shapes=[
             pltpu.VMEM((owned, width), bf16),
-            pltpu.VMEM((shard_rows, width), bf16),
-            pltpu.VMEM((shards, tokens, shard_rows), bf16),
+            pltpu.VMEM((shards * shard_rows, width), bf16),
+            pltpu.VMEM((tokens, shards * shard_rows), bf16),
             pltpu.VMEM((chunks, shards * tokens, rows), bf16),
             pltpu.VMEM((shards * tokens, width), bf16),
             pltpu.VMEM((chunks, rows, width), f32),
@@ -276,12 +316,16 @@
             dma(()),
             dma((shards,)),
             dma((shards,)),
+            dma((shards, replicas // 2)),
+            dma((shards, replicas // 2)),
+            dma((shards, replicas // 2)),
+            dma((shards, replicas // 2)),
             dma(()),
             dma((replicas,)),
             dma((replicas,)),
         ],
         compiler_params=pltpu.CompilerParams(
-            collective_id=0, has_side_effects=True, vmem_limit_bytes=58 * 2**20
+            collective_id=0, has_side_effects=True, vmem_limit_bytes=60 * 2**20
         ),
         cost_estimate=pl.CostEstimate(
             flops=2 * tokens * shards * shard_rows * width,

time: 266 us -> 288 us (1.083)
  Pallas kernels: 251 us -> 273 us
    pallas_call x1, Pallas kernels: 251 us -> 273 us  [exchange(): pl.pallas_call(functools.partial(exchange_kernel, shards, replicas), in_s...]
where the time goes in v3:
time: 288 us; the launch traced here: 287 us
  Pallas kernels  273 us (95%)
  local copies, waits for them, and re-layouts  13.5 us (5%)
    pallas_call x1, Pallas kernels, exchange(): pl.pallas_call(functools.partial(exchange_kernel, shards, replicas), in_s...  273 us
    unnamed x12, local copies, waits for them, and re-layouts  13.5 us

profile of v3, /device:TPU:27, one launch (start us, length us, event | category | flops | bytes accessed | tf_op | source)
XLA Modules:
  0.0 286.7 jit_solution(14474339177828745457)
XLA Ops:
  0.6 272.5 %shard_map.93 = (bf16[256,8192]{1,0:T(8,128)(2,1)}, bf16[2048,1024]{1,0:T(8,128)(2,1)}, f32[1,2048,1024]{2,1,0:T(8,128)}, f32[1,256,1024]{2,1,0:T(8,128)}) custom-call(bf16[256,8192]{1,0:T(8,128)(2,1)} %features.1, bf16[256,1024]{1,0:T(8,128)(2,1)} %grads.1, bf16[2048,1024]{1,0:T(8,128)(2,1)} %weight.1, f32[1,2048,1024]{2,1,0:T(8,128)} %moment.1, ...), custom_call_target="tpu_custom_call" | custom-call | flops 4294967296 | bytes 251658240 | tf_op jit(solution)/shard_map/pallas_call | solution.py:285
  273.2 0.0 copy-start
  273.2 0.0 slice-start
  273.2 4.9 %copy.14 = bf16[256,8192]{1,0:T(8,128)(2,1)} copy(bf16[256,8192]{1,0:T(8,128)(2,1)} %get-tuple-element.8) | data formatting | bytes 8388608
  278.1 0.0 copy-done
  278.1 0.0 slice-start.1
  278.1 2.1 copy.15
  280.2 0.0 slice-done
  280.2 2.1 slice-done.1
  282.3 0.0 copy-start.1
  282.3 3.4 %copy.16 = f32[1,2048,1024]{2,1,0:T(8,128)} copy(f32[1,2048,1024]{2,1,0:T(8,128)S(1)} %bitcast.1) | data formatting | bytes 16777216
  285.7 0.0 copy-done.1
  285.7 1.0 copy.17
  (1 shorter events, 0.0 us)
Async XLA Ops:
  273.2 4.9 %copy-start = (bf16[2048,1024]{1,0:T(8,128)(2,1)S(1)}, bf16[2048,1024]{1,0:T(8,128)(2,1)}, u32[]{:S(2)}) copy-start(bf16[2048,1024]{1,0:T(8,128)(2,1)} %get-tuple-element.9) | copy-start | bytes 12582916
  273.2 7.1 %slice-start = ((s8[8388608]{0:T(1024)(128)(4,1)}), s8[4194304]{0:T(1024)(128)(4,1)S(1)}, s32[]{:S(2)}) async-start(s8[8388608]{0:T(1024)(128)(4,1)} %bitcast), calls=%async_computation | async-start | bytes 8388608
  278.1 4.2 %slice-start.1 = ((s8[8388608]{0:T(1024)(128)(4,1)}), s8[4194304]{0:T(1024)(128)(4,1)S(1)}, s32[]{:S(2)}) async-start(s8[8388608]{0:T(1024)(128)(4,1)} %bitcast), calls=%async_computation.1 | async-start | bytes 8388608
  282.3 3.4 %copy-start.1 = (f32[1,256,1024]{2,1,0:T(8,128)S(1)}, f32[1,256,1024]{2,1,0:T(8,128)}, u32[]{:S(2)}) copy-start(f32[1,256,1024]{2,1,0:T(8,128)} %get-tuple-element.11) | copy-start | bytes 3145732
